TPU v7x, 512 devices: a whole 4x4x16 slice. The times are simulated.
512 devices in a mesh: row: 32 (over z, core), col: 16 (over y, x).
Axes of the slice: x: 4, y: 4, z: 16, core: 2. Of those that a mesh axis runs over, the one named last changes fastest.
Arguments:
- flow_tiles: bfloat16 [32, 32, 256, 256], P('row', 'col'), may hold values from 0.1 to 25
- tile_cols: int32 [32, 32], P('row', 'col'), may hold values from -1 to 31, as said below
- pairs: int32 [32768, 2], P(('row', 'col')), may hold values from -1 to 31, as said below
Outputs:
- new_flow: float32 [32, 32, 256, 256], P('row', 'col')
Inputs may be any that keep to these rules, and one draw needn't show every extreme that they name: `tile_cols`: the stored slots of device (r, c) have distinct tile columns, each congruent to c modulo the col axis's size; tile row r stores tile column r. `pairs`: device (r, c) lists, in some order and without repeats, exactly the (k, s) for which slot s of the device is stored and M[r, k] and M[k, tile_cols[r, c * 2 + s]] are both stored tiles; its other rows are (-1, -1). Some device uses all 64 rows.
All inputs are finite; a program needn't handle non-finite values.
Results may differ from a plain program's by a relative error of at most 0.0003.
Values may be sent and summed in bfloat16 or wider, within the bound.
No kernel may reach another device: no remote copies, remote signals or barrier semaphores. Data moves between devices by JAX's collectives and lax.ppermute only.
A program may use at most 64 MiB of HBM per device.

v0:
```python
import jax
import jax.numpy as jnp
from jax import lax
from jax.sharding import PartitionSpec as P


def copy_for_each(shard, axis):
    length = lax.axis_size(axis)
    return lax.all_to_all(
        jnp.broadcast_to(shard[None], (length, *shard.shape)), axis, 0, 0, tiled=True
    )


def over_copies(shard, axis):
    return copy_for_each(shard, axis).sum(axis=0)


def block_products(
    initial, left_source, right_source, left_index, right_row, right_slot, weight, groups
):
    tile_count = weight.shape[1]
    left_index = left_index.reshape(groups, -1)
    right_row = right_row.reshape(groups, -1)
    right_slot = right_slot.reshape(groups, -1)
    weight = weight.reshape(groups, -1, tile_count)

    def block_step(carried, inputs):
        left_pick, row_pick, slot_pick, weight_block = inputs
        left_tiles = left_source[left_pick]
        right_tiles = right_source[row_pick, slot_pick]
        products = jnp.einsum(
            "pab,pbc->pac", left_tiles, right_tiles, preferred_element_type=jnp.float32
        )
        added = jnp.einsum("ps,pac->sac", weight_block, products, precision=lax.Precision.HIGHEST)
        return (carried + added, None)

    result, unused = lax.scan(block_step, initial, (left_index, right_row, right_slot, weight))
    return result


def on_device(flow_tiles, tile_cols, pairs):
    tile_count = flow_tiles.shape[1]
    tile_width = flow_tiles.shape[3]
    col_count = lax.axis_size("col")
    rows_total = lax.axis_size("row") * tile_width
    col_index = lax.axis_index("col")
    row_tiles, row_cols = (
        lax.all_gather(flow_tiles, "col", axis=1, tiled=True),
        lax.all_gather(tile_cols, "col", axis=1, tiled=True),
    )
    own_cols = tile_cols[0]
    inner_tile = pairs[:, 0]
    slot_list = pairs[:, 1]
    is_live = inner_tile >= 0
    inner_safe = jnp.maximum(inner_tile, 0)
    slot_safe = jnp.maximum(slot_list, 0)
    wanted = own_cols[slot_safe]
    left_index = jnp.argmax(row_cols[0][None, :] == inner_safe[:, None], axis=1)
    slot_ids = jnp.arange(tile_count, dtype=jnp.int32)
    weight = (is_live[:, None] & (slot_list[:, None] == slot_ids[None, :])).astype(jnp.float32)
    initial = jnp.zeros((tile_count, tile_width, tile_width), jnp.float32)
    column_tiles, column_cols = (
        lax.all_gather(flow_tiles, "row", axis=0, tiled=True),
        lax.all_gather(tile_cols, "row", axis=0, tiled=True),
    )
    right_slot = jnp.argmax(column_cols[inner_safe] == wanted[:, None], axis=1)
    expanded = block_products(
        initial, row_tiles[0], column_tiles, left_index, inner_safe, right_slot, weight, 4
    )
    inflated = expanded * expanded
    partial_sums = jnp.sum(inflated, axis=1)
    targets = col_index + col_count * slot_ids
    matches = own_cols[None, :] == targets[:, None]
    canonical = jnp.sum(jnp.where(matches[:, :, None], partial_sums[None, :, :], 0.0), axis=1)
    totals = over_copies(canonical, "row")
    per_slot = jnp.sum(jnp.where(matches[:, :, None], totals[:, None, :], 0.0), axis=0)
    stored = own_cols >= 0
    per_slot = jnp.where(stored[:, None], per_slot, 1.0)
    normed = inflated * jnp.float32(rows_total) / per_slot[:, None, :]
    blended = 0.5 * flow_tiles[0].astype(jnp.float32) + 0.5 * normed
    blended = jnp.where(stored[:, None, None], blended, 0.0)
    return blended[None]


def solution(mesh):
    placed = (P("row", "col", None, None), P("row", "col"), P(("row", "col"), None))
    return jax.shard_map(
        on_device,
        mesh=mesh,
        in_specs=placed,
        out_specs=P("row", "col", None, None),
        check_vma=False,
    )
```

profile of v0, /device:TPU:2, one launch (start us, length us, event | category | flops | bytes accessed | tf_op | source)
XLA Modules:
  0.0 273.3 jit_solution(3193878392183024058)
XLA Ops:
  6.5 0.0 all-gather.4.cloned.1.call-start
  6.5 0.7 all-gather.4.cloned.1.call-update
  7.3 0.0 all-gather.6.cloned.1.call-start
  7.3 0.7 all-gather.6.cloned.1.call-update
  8.0 36.2 %all-gather = s32[32,1,2]{2,1,0:T(1,128)S(1)} all-gather(s32[1,1,2]{2,1,0:T(1,128)} %bitcast.62), channel_id=1, replica_groups=mesh['row'=32,'col'=16] {'row'}, dimensions={0}, use_global_device_ids=true | all-gather | bytes 264 | tf_op jit(solution)/shard_map/all_gather | solution.py:64
  44.3 1.3 fusion.17
  45.6 2.0 maximum_reduce_fusion
  47.6 0.6 gather_fusion.2
  48.2 0.7 iota_reduce_fusion
  48.9 0.1 reshape.172
  49.0 1.3 dynamic-slice
  50.9 0.8 bitcast_dynamic-update-slice_fusion
  51.6 15.7 %all-reduce = s32[32]{0:T(128)S(1)} all-reduce(s32[32]{0:T(128)S(1)} %bitcast_dynamic-update-slice_fusion), channel_id=1, replica_groups=mesh['row'=32,'col'=16] {'col'}, use_global_device_ids=true, to_apply=%add | all-reduce | flops 32 | bytes 256
  67.4 0.6 iota_reduce_fusion.1
  68.0 0.1 reshape.171
  68.1 0.1 eq.62
  68.2 0.7 compare_reduce_fusion
  68.9 0.1 and.16
  69.0 0.1 max.14
  69.1 0.7 broadcast_compare_fusion
  69.8 11.9 %all-gather.4.cloned.1.call-done = bf16[1,32,256,256]{3,2,0,1:T(8,128)(2,1)} async-done(((bf16[1,2,256,256]{3,2,0,1:T(8,128)(2,1)}), bf16[1,32,256,256]{3,2,0,1:T(8,128)(2,1)}) %all-gather.4.cloned.1.call-update) | async-done | bytes 4194320 | tf_op jit(solution)/shard_map/all_gather | solution.py:48
  81.7 81.5 %all-gather.6.cloned.1.call-done = bf16[32,2,256,256]{3,2,1,0:T(8,128)(2,1)} async-done(((bf16[1,2,256,256]{3,2,1,0:T(8,128)(2,1)}), bf16[32,2,256,256]{3,2,1,0:T(8,128)(2,1)}) %all-gather.6.cloned.1.call-update) | async-done | bytes 8388624 | tf_op jit(solution)/shard_map/all_gather | solution.py:63
  163.2 79.1 %while.11 = (s32[]{:T(128)}, f32[2,256,256]{2,0,1:T(2,128)S(1)}, f32[4,16,2]{1,2,0:T(2,128)S(1)}, s32[4,16]{1,0:T(4,128)S(1)}, bf16[32,256,256]{2,1,0:T(8,128)(2...) while((s32[]{:T(128)}, f32[2,256,256]{2,0,1:T(2,128)S(1)}, ...), condition=%wide.region_3.4_spmd.clone, body=%wide.region_2.3_spmd.clone.sunk | while | flops 562300160 | bytes 22025908 | solution.py:37
  163.2 2.9 %gather_fusion = bf16[16,256,256]{2,1,0:T(8,128)(2,1)S(1)} fusion(bf16[32,256,256]{2,1,0:T(8,128)(2,1)} %get-tuple-element.180, s32[1024]{0:T(1024)S(1)} %pad_clamp_fusion.3), kind=kCustom, calls=%fused_computation.clone.clone.1 | custom fusion | bytes 4194368 | tf_op jit(solution)/shard_map/while/body/eval_jaxpr/gather | solution.py:29
  166.2 5.4 %gather_fusion.1 = bf16[16,256,256]{2,1,0:T(8,128)(2,1)} fusion(bf16[32,2,256,256]{3,2,1,0:T(8,128)(2,1)} %get-tuple-element.183, s32[16]{0:T(128)S(1)} %get-tuple-element.155), kind=kCustom, calls=%fused_computation.1.clone.clone.1 | custom fusion | bytes 4194432 | tf_op jit(solution)/shard_map/while/body/eval_jaxpr/gather | solution.py:30
  171.6 4.3 %fusion.31 = f32[16,256,256]{2,1,0:T(8,128)} fusion(bf16[16,256,256]{2,1,0:T(8,128)(2,1)S(1)} %gather_fusion, bf16[16,256,256]{2,1,0:T(8,128)(2,1)} %gather_fusion.1), kind=kOutput, calls=%fused_computation.45.clone.1 | convolution fusion | flops 536870912 | bytes 8388608 | tf_op jit(solution)/shard_map/while/body/eval_jaxpr/pab,pbc->pac/dot_general | solution.py:31
  175.8 7.2 %fusion.32 = f32[2,256,256]{2,0,1:T(2,128)S(1)} fusion(f32[16,256,256]{2,1,0:T(8,128)} %fusion.31, f32[2,256,256]{2,0,1:T(2,128)S(1)} %get-tuple-element.167, pred[]{:T(512)S(6)} %compare.10, f32[4,16,2]{1,2,0:T(2,128)S(1)} %get-tuple-element.178, s32[]{:T(128)} %get-tuple-element.166), kind=kOutput, calls=%fused_computation.5.clone.1 | convolution fusion | flops 25427968 | bytes 5243909 | tf_op jit(solution)/shard_map/while/body/eval_jaxpr/ps,pac->sac/dot_general | solution.py:34
  183.1 2.9 %gather_fusion = bf16[16,256,256]{2,1,0:T(8,128)(2,1)S(1)} fusion(bf16[32,256,256]{2,1,0:T(8,128)(2,1)} %get-tuple-element.180, s32[1024]{0:T(1024)S(1)} %pad_clamp_fusion.3), kind=kCustom, calls=%fused_computation.clone.clone.1 | custom fusion | bytes 4194368 | tf_op jit(solution)/shard_map/while/body/eval_jaxpr/gather | solution.py:29
  185.9 5.4 %gather_fusion.1 = bf16[16,256,256]{2,1,0:T(8,128)(2,1)} fusion(bf16[32,2,256,256]{3,2,1,0:T(8,128)(2,1)} %get-tuple-element.183, s32[16]{0:T(128)S(1)} %get-tuple-element.155), kind=kCustom, calls=%fused_computation.1.clone.clone.1 | custom fusion | bytes 4194432 | tf_op jit(solution)/shard_map/while/body/eval_jaxpr/gather | solution.py:30
  191.3 4.3 %fusion.31 = f32[16,256,256]{2,1,0:T(8,128)} fusion(bf16[16,256,256]{2,1,0:T(8,128)(2,1)S(1)} %gather_fusion, bf16[16,256,256]{2,1,0:T(8,128)(2,1)} %gather_fusion.1), kind=kOutput, calls=%fused_computation.45.clone.1 | convolution fusion | flops 536870912 | bytes 8388608 | tf_op jit(solution)/shard_map/while/body/eval_jaxpr/pab,pbc->pac/dot_general | solution.py:31
  195.6 7.2 %fusion.32 = f32[2,256,256]{2,0,1:T(2,128)S(1)} fusion(f32[16,256,256]{2,1,0:T(8,128)} %fusion.31, f32[2,256,256]{2,0,1:T(2,128)S(1)} %get-tuple-element.167, pred[]{:T(512)S(6)} %compare.10, f32[4,16,2]{1,2,0:T(2,128)S(1)} %get-tuple-element.178, s32[]{:T(128)} %get-tuple-element.166), kind=kOutput, calls=%fused_computation.5.clone.1 | convolution fusion | flops 25427968 | bytes 5243909 | tf_op jit(solution)/shard_map/while/body/eval_jaxpr/ps,pac->sac/dot_general | solution.py:34
  202.8 2.9 %gather_fusion = bf16[16,256,256]{2,1,0:T(8,128)(2,1)S(1)} fusion(bf16[32,256,256]{2,1,0:T(8,128)(2,1)} %get-tuple-element.180, s32[1024]{0:T(1024)S(1)} %pad_clamp_fusion.3), kind=kCustom, calls=%fused_computation.clone.clone.1 | custom fusion | bytes 4194368 | tf_op jit(solution)/shard_map/while/body/eval_jaxpr/gather | solution.py:29
  205.7 5.4 %gather_fusion.1 = bf16[16,256,256]{2,1,0:T(8,128)(2,1)} fusion(bf16[32,2,256,256]{3,2,1,0:T(8,128)(2,1)} %get-tuple-element.183, s32[16]{0:T(128)S(1)} %get-tuple-element.155), kind=kCustom, calls=%fused_computation.1.clone.clone.1 | custom fusion | bytes 4194432 | tf_op jit(solution)/shard_map/while/body/eval_jaxpr/gather | solution.py:30
  211.1 4.3 %fusion.31 = f32[16,256,256]{2,1,0:T(8,128)} fusion(bf16[16,256,256]{2,1,0:T(8,128)(2,1)S(1)} %gather_fusion, bf16[16,256,256]{2,1,0:T(8,128)(2,1)} %gather_fusion.1), kind=kOutput, calls=%fused_computation.45.clone.1 | convolution fusion | flops 536870912 | bytes 8388608 | tf_op jit(solution)/shard_map/while/body/eval_jaxpr/pab,pbc->pac/dot_general | solution.py:31
  215.4 7.2 %fusion.32 = f32[2,256,256]{2,0,1:T(2,128)S(1)} fusion(f32[16,256,256]{2,1,0:T(8,128)} %fusion.31, f32[2,256,256]{2,0,1:T(2,128)S(1)} %get-tuple-element.167, pred[]{:T(512)S(6)} %compare.10, f32[4,16,2]{1,2,0:T(2,128)S(1)} %get-tuple-element.178, s32[]{:T(128)} %get-tuple-element.166), kind=kOutput, calls=%fused_computation.5.clone.1 | convolution fusion | flops 25427968 | bytes 5243909 | tf_op jit(solution)/shard_map/while/body/eval_jaxpr/ps,pac->sac/dot_general | solution.py:34
  222.6 2.9 %gather_fusion = bf16[16,256,256]{2,1,0:T(8,128)(2,1)S(1)} fusion(bf16[32,256,256]{2,1,0:T(8,128)(2,1)} %get-tuple-element.180, s32[1024]{0:T(1024)S(1)} %pad_clamp_fusion.3), kind=kCustom, calls=%fused_computation.clone.clone.1 | custom fusion | bytes 4194368 | tf_op jit(solution)/shard_map/while/body/eval_jaxpr/gather | solution.py:29
  225.5 5.4 %gather_fusion.1 = bf16[16,256,256]{2,1,0:T(8,128)(2,1)} fusion(bf16[32,2,256,256]{3,2,1,0:T(8,128)(2,1)} %get-tuple-element.183, s32[16]{0:T(128)S(1)} %get-tuple-element.155), kind=kCustom, calls=%fused_computation.1.clone.clone.1 | custom fusion | bytes 4194432 | tf_op jit(solution)/shard_map/while/body/eval_jaxpr/gather | solution.py:30
  230.9 4.3 %fusion.31 = f32[16,256,256]{2,1,0:T(8,128)} fusion(bf16[16,256,256]{2,1,0:T(8,128)(2,1)S(1)} %gather_fusion, bf16[16,256,256]{2,1,0:T(8,128)(2,1)} %gather_fusion.1), kind=kOutput, calls=%fused_computation.45.clone.1 | convolution fusion | flops 536870912 | bytes 8388608 | tf_op jit(solution)/shard_map/while/body/eval_jaxpr/pab,pbc->pac/dot_general | solution.py:31
  235.2 7.2 %fusion.32 = f32[2,256,256]{2,0,1:T(2,128)S(1)} fusion(f32[16,256,256]{2,1,0:T(8,128)} %fusion.31, f32[2,256,256]{2,0,1:T(2,128)S(1)} %get-tuple-element.167, pred[]{:T(512)S(6)} %compare.10, f32[4,16,2]{1,2,0:T(2,128)S(1)} %get-tuple-element.178, s32[]{:T(128)} %get-tuple-element.166), kind=kOutput, calls=%fused_computation.5.clone.1 | convolution fusion | flops 25427968 | bytes 5243909 | tf_op jit(solution)/shard_map/while/body/eval_jaxpr/ps,pac->sac/dot_general | solution.py:34
  242.3 0.1 fusion.15
  242.4 0.1 select_reduce_fusion.1
  242.5 0.7 broadcast_in_dim.93
  243.2 7.8 %all-to-all-start = ((f32[32,2,256]{2,1,0:T(2,128)}), f32[32,2,256]{2,1,0:T(2,128)S(1)}, u32[]{:S(2)}, u32[]{:S(2)}) async-start(f32[32,2,256]{2,1,0:T(2,128)} %broadcast_in_dim.93), calls=%async_computation | async-start | bytes 131072 | tf_op jit(solution)/shard_map/all_to_all | solution.py:9
  250.9 0.0 copy-done.1
  250.9 14.4 %all-to-all-done = f32[32,2,256]{2,1,0:T(2,128)S(1)} async-done(((f32[32,2,256]{2,1,0:T(2,128)}), f32[32,2,256]{2,1,0:T(2,128)S(1)}, u32[]{:S(2)}, u32[]{:S(2)}) %all-to-all-start) | async-done | bytes 65568 | tf_op jit(solution)/shard_map/all_to_all | solution.py:9
  265.4 0.1 select_reduce_fusion
  265.5 0.1 broadcast_select_fusion
  265.5 0.9 fusion.14
  (18 shorter events, 0.2 us)
Async XLA Ops:
  6.5 75.2 %all-gather.4.cloned.1.call-start = ((), (), s32[]{:S(2)}) async-start(), calls=%async_computation.1 | async-start | bytes 4456448 | tf_op jit(solution)/shard_map/all_gather | solution.py:48
  7.3 156.0 %all-gather.6.cloned.1.call-start = ((), (), s32[]{:S(2)}) async-start(), calls=%async_computation.2 | async-start | bytes 8650752 | tf_op jit(solution)/shard_map/all_gather | solution.py:63
  163.2 87.7 %copy-start.1 = (s32[1,2]{1,0:T(1,128)S(1)}, s32[1,2]{1,0:T(1,128)}, u32[]{:S(2)}) copy-start(s32[1,2]{1,0:T(1,128)} %param.6) | copy-start | bytes 28
  163.2 102.3 %copy-start = (bf16[1,2,256,256]{3,2,1,0:T(8,128)(2,1)S(1)}, bf16[1,2,256,256]{3,2,1,0:T(8,128)(2,1)}, u32[]{:S(2)}) copy-start(bf16[1,2,256,256]{3,2,1,0:T(8,128)(2,1)} %param.5) | copy-start | bytes 786436
  243.2 22.2 %all-to-all-start = ((f32[32,2,256]{2,1,0:T(2,128)}), f32[32,2,256]{2,1,0:T(2,128)S(1)}, u32[]{:S(2)}, u32[]{:S(2)}) async-start(f32[32,2,256]{2,1,0:T(2,128)} %broadcast_in_dim.93), calls=%async_computation | async-start | bytes 131072 | tf_op jit(solution)/shard_map/all_to_all | solution.py:9
Sparse Core Ops, SparseCore 0:
  10.4 71.3 all-gather.3
  83.9 79.2 all-gather.5
where the time goes:
time: 274 us; the launch traced here: 273 us
  waiting for transfers between devices  109 us (40%)
  blocking collectives  52 us (19%)
  matrix products  45.8 us (17%)
  local copies, waits for them, and re-layouts  38.2 us (14%)
  between operations  14.1 us (5%)
  starting transfers between devices  7.8 us (3%)
  other arithmetic  6.17 us (2%)
    all_gather x1, waiting for transfers between devices, on_device(): lax.all_gather(flow_tiles, 'row', axis=0, tiled=True)  81.5 us
    all_gather x1, blocking collectives, on_device(): lax.all_gather(tile_cols, 'row', axis=0, tiled=True)  36.2 us
    dot_general x4, matrix products, block_step(): jnp.einsum('ps,pac->sac', weight_block, products, precision=lax.Precision...  28.7 us
    gather x4, local copies, waits for them, and re-layouts, block_step(): right_tiles = right_source[row_pick, slot_pick]  21.7 us
    dot_general x4, matrix products, block_step(): jnp.einsum('pab,pbc->pac', left_tiles, right_tiles, preferred_element_typ...  17 us
    unnamed x1, blocking collectives  15.7 us
    all_to_all x1, waiting for transfers between devices, copy_for_each(): lax.all_to_all(jnp.broadcast_to(shard[None], (length, *shard.shape)), axi...  14.4 us
    all_gather x1, waiting for transfers between devices, on_device(): lax.all_gather(flow_tiles, 'col', axis=1, tiled=True)  11.9 us
  transfers between devices with their start and end apart: 3, of which 3 were waited for; matrix products, arithmetic and copies ran while one was open for 3% of the time, Pallas kernels for 0%

commit v1 on v0

--- a/solution.py
+++ b/solution.py
@@ -45,7 +45,9 @@
     rows_total = lax.axis_size("row") * tile_width
     col_index = lax.axis_index("col")
     row_tiles, row_cols = (
-        lax.all_gather(flow_tiles, "col", axis=1, tiled=True),
+        jnp.concatenate(
+            lax.all_to_all(jnp.stack([flow_tiles] * lax.axis_size("col")), "col", 0, 0), axis=1
+        ),
         lax.all_gather(tile_cols, "col", axis=1, tiled=True),
     )
     own_cols = tile_cols[0]

time: 274 us -> 208 us (0.76)
  waiting for transfers between devices: 109 us -> 25.2 us
  starting transfers between devices: 7.8 us -> 21.5 us
  blocking collectives: 52 us -> 55.9 us
    all_gather x1, waiting for transfers between devices: 81.5 us -> 10.1 us  [on_device(): lax.all_gather(flow_tiles, 'row', axis=0, tiled=True)]
    all_gather x1 -> x0, waiting for transfers between devices: 11.9 us -> none  [on_device(): lax.all_gather(flow_tiles, 'col', axis=1, tiled=True)]
    all_to_all x0 -> x1, starting transfers between devices: none -> 10.3 us  [on_device(): lax.all_to_all(jnp.stack([flow_tiles] * lax.axis_size('col')), 'col', 0, 0)]
    unnamed x1, blocking collectives: 15.7 us -> 22.6 us
    all_to_all x1, starting transfers between devices: 7.75 us -> 11.2 us  [copy_for_each(): lax.all_to_all(jnp.broadcast_to(shard[None], (length, *shard.shape)), axi...]
    another operation x0 -> x1, local copies, waits for them, and re-layouts: none -> 3.38 us  [on_device(): jnp.stack([flow_tiles] * lax.axis_size('col'))]
    all_gather x1, blocking collectives: 36.2 us -> 33.4 us  [on_device(): lax.all_gather(tile_cols, 'row', axis=0, tiled=True)]
  transfers between devices with their start and end apart: 3 -> 3, of which waited for: 3 -> 2; matrix products, arithmetic and copies ran while one was open for 3% -> 4% of each run, Pallas kernels for 0% -> 0%
where the time goes in v1:
time: 208 us; the launch traced here: 207 us
  blocking collectives  55.9 us (27%)
  matrix products  45.8 us (22%)
  local copies, waits for them, and re-layouts  40.2 us (19%)
  waiting for transfers between devices  25.2 us (12%)
  starting transfers between devices  21.5 us (10%)
  between operations  14 us (7%)
  other arithmetic  4.01 us (2%)
    all_gather x1, blocking collectives, on_device(): lax.all_gather(tile_cols, 'row', axis=0, tiled=True)  33.4 us
    dot_general x4, matrix products, block_step(): jnp.einsum('ps,pac->sac', weight_block, products, precision=lax.Precision...  28.7 us
    unnamed x1, blocking collectives  22.6 us
    gather x4, local copies, waits for them, and re-layouts, block_step(): right_tiles = right_source[row_pick, slot_pick]  21.7 us
    dot_general x4, matrix products, block_step(): jnp.einsum('pab,pbc->pac', left_tiles, right_tiles, preferred_element_typ...  17 us
    all_to_all x1, waiting for transfers between devices, copy_for_each(): lax.all_to_all(jnp.broadcast_to(shard[None], (length, *shard.shape)), axi...  14.4 us
    gather x4, local copies, waits for them, and re-layouts, block_step(): left_tiles = left_source[left_pick]  11.5 us
    all_to_all x1, starting transfers between devices, copy_for_each(): lax.all_to_all(jnp.broadcast_to(shard[None], (length, *shard.shape)), axi...  11.2 us
  transfers between devices with their start and end apart: 3, of which 2 were waited for; matrix products, arithmetic and copies ran while one was open for 4% of the time, Pallas kernels for 0%

profile of v1, /device:TPU:2, one launch (start us, length us, event | category | flops | bytes accessed | tf_op | source)
XLA Modules:
  0.0 206.8 jit_solution(8213955774099644570)
XLA Ops:
  6.5 0.0 all-gather.3.cloned.1.call-start
  6.5 0.7 all-gather.3.cloned.1.call-update
  7.3 3.4 %stack.2 = bf16[16,1,2,256,256]{4,3,2,1,0:T(8,128)(2,1)} broadcast(bf16[2,256,256]{2,1,0:T(8,128)(2,1)} %bitcast.58), dimensions={2,3,4} | broadcast | bytes 4456448 | tf_op jit(solution)/shard_map/stack | solution.py:49
  10.6 10.3 %all-to-all-start = ((bf16[16,1,2,256,256]{4,3,2,1,0:T(8,128)(2,1)}), bf16[16,1,2,256,256]{4,3,2,1,0:T(8,128)(2,1)}, u32[]{:S(2)}, u32[]{:S(2)}) async-start(bf16[16,1,2,256,256]{4,3,2,1,0:T(8,128)(2,1)} %stack.2), calls=%async_computation | async-start | bytes 8388608 | tf_op jit(solution)/shard_map/all_to_all | solution.py:49
  21.0 33.4 %all-gather = s32[32,1,2]{2,1,0:T(1,128)S(1)} all-gather(s32[1,1,2]{2,1,0:T(1,128)S(1)} %bitcast.59), channel_id=1, replica_groups=mesh['row'=32,'col'=16] {'row'}, dimensions={0}, use_global_device_ids=true | all-gather | bytes 264 | tf_op jit(solution)/shard_map/all_gather | solution.py:66
  54.3 0.6 fusion.14
  54.9 0.0 copy-done.2
  54.9 1.2 maximum_reduce_fusion
  56.2 0.6 gather_fusion.2
  56.8 0.7 iota_reduce_fusion
  57.5 0.1 reshape.173
  57.5 1.3 dynamic-slice
  59.4 0.1 bitcast_dynamic-update-slice_fusion
  59.5 22.6 %all-reduce = s32[32]{0:T(128)S(1)} all-reduce(s32[32]{0:T(128)S(1)} %bitcast_dynamic-update-slice_fusion), channel_id=1, replica_groups=mesh['row'=32,'col'=16] {'col'}, use_global_device_ids=true, to_apply=%add | all-reduce | flops 32 | bytes 256
  82.0 0.6 iota_reduce_fusion.1
  82.6 0.1 reshape.172
  82.7 0.1 eq.62
  82.8 0.1 and.16
  82.9 0.1 max.14
  83.0 0.1 broadcast_compare_fusion
  83.1 0.0 all-to-all-done
  83.1 10.1 %all-gather.3.cloned.1.call-done = bf16[32,2,256,256]{3,2,1,0:T(8,128)(2,1)} async-done(((bf16[1,2,256,256]{3,2,1,0:T(8,128)(2,1)}), bf16[32,2,256,256]{3,2,1,0:T(8,128)(2,1)}) %all-gather.3.cloned.1.call-update) | async-done | bytes 8388624 | tf_op jit(solution)/shard_map/all_gather | solution.py:65
  93.2 79.1 %while.11 = (s32[]{:T(128)}, f32[2,256,256]{2,0,1:T(2,128)S(1)}, f32[4,16,2]{1,2,0:T(2,128)S(1)}, s32[4,16]{1,0:T(4,128)S(1)}, bf16[32,256,256]{2,1,0:T(8,128)(2...) while((s32[]{:T(128)}, f32[2,256,256]{2,0,1:T(2,128)S(1)}, ...), condition=%wide.region_3.4_spmd.clone, body=%wide.region_2.3_spmd.clone.sunk | while | flops 562300160 | bytes 22025908 | solution.py:37
  93.3 2.9 %gather_fusion = bf16[16,256,256]{2,1,0:T(8,128)(2,1)S(1)} fusion(bf16[32,256,256]{2,1,0:T(8,128)(2,1)} %get-tuple-element.180, s32[1024]{0:T(1024)S(1)} %pad_clamp_fusion.3), kind=kCustom, calls=%fused_computation.clone.clone.1 | custom fusion | bytes 4194368 | tf_op jit(solution)/shard_map/while/body/eval_jaxpr/gather | solution.py:29
  96.2 5.4 %gather_fusion.1 = bf16[16,256,256]{2,1,0:T(8,128)(2,1)} fusion(bf16[32,2,256,256]{3,2,1,0:T(8,128)(2,1)} %get-tuple-element.183, s32[16]{0:T(128)S(1)} %get-tuple-element.155), kind=kCustom, calls=%fused_computation.1.clone.clone.1 | custom fusion | bytes 4194432 | tf_op jit(solution)/shard_map/while/body/eval_jaxpr/gather | solution.py:30
  101.6 4.3 %fusion.28 = f32[16,256,256]{2,1,0:T(8,128)} fusion(bf16[16,256,256]{2,1,0:T(8,128)(2,1)S(1)} %gather_fusion, bf16[16,256,256]{2,1,0:T(8,128)(2,1)} %gather_fusion.1), kind=kOutput, calls=%fused_computation.42.clone.1 | convolution fusion | flops 536870912 | bytes 8388608 | tf_op jit(solution)/shard_map/while/body/eval_jaxpr/pab,pbc->pac/dot_general | solution.py:31
  105.9 7.2 %fusion.29 = f32[2,256,256]{2,0,1:T(2,128)S(1)} fusion(f32[16,256,256]{2,1,0:T(8,128)} %fusion.28, f32[2,256,256]{2,0,1:T(2,128)S(1)} %get-tuple-element.167, pred[]{:T(512)S(6)} %compare.10, f32[4,16,2]{1,2,0:T(2,128)S(1)} %get-tuple-element.178, s32[]{:T(128)} %get-tuple-element.166), kind=kOutput, calls=%fused_computation.5.clone.1 | convolution fusion | flops 25427968 | bytes 5243909 | tf_op jit(solution)/shard_map/while/body/eval_jaxpr/ps,pac->sac/dot_general | solution.py:34
  113.1 2.9 %gather_fusion = bf16[16,256,256]{2,1,0:T(8,128)(2,1)S(1)} fusion(bf16[32,256,256]{2,1,0:T(8,128)(2,1)} %get-tuple-element.180, s32[1024]{0:T(1024)S(1)} %pad_clamp_fusion.3), kind=kCustom, calls=%fused_computation.clone.clone.1 | custom fusion | bytes 4194368 | tf_op jit(solution)/shard_map/while/body/eval_jaxpr/gather | solution.py:29
  116.0 5.4 %gather_fusion.1 = bf16[16,256,256]{2,1,0:T(8,128)(2,1)} fusion(bf16[32,2,256,256]{3,2,1,0:T(8,128)(2,1)} %get-tuple-element.183, s32[16]{0:T(128)S(1)} %get-tuple-element.155), kind=kCustom, calls=%fused_computation.1.clone.clone.1 | custom fusion | bytes 4194432 | tf_op jit(solution)/shard_map/while/body/eval_jaxpr/gather | solution.py:30
  121.4 4.3 %fusion.28 = f32[16,256,256]{2,1,0:T(8,128)} fusion(bf16[16,256,256]{2,1,0:T(8,128)(2,1)S(1)} %gather_fusion, bf16[16,256,256]{2,1,0:T(8,128)(2,1)} %gather_fusion.1), kind=kOutput, calls=%fused_computation.42.clone.1 | convolution fusion | flops 536870912 | bytes 8388608 | tf_op jit(solution)/shard_map/while/body/eval_jaxpr/pab,pbc->pac/dot_general | solution.py:31
  125.6 7.2 %fusion.29 = f32[2,256,256]{2,0,1:T(2,128)S(1)} fusion(f32[16,256,256]{2,1,0:T(8,128)} %fusion.28, f32[2,256,256]{2,0,1:T(2,128)S(1)} %get-tuple-element.167, pred[]{:T(512)S(6)} %compare.10, f32[4,16,2]{1,2,0:T(2,128)S(1)} %get-tuple-element.178, s32[]{:T(128)} %get-tuple-element.166), kind=kOutput, calls=%fused_computation.5.clone.1 | convolution fusion | flops 25427968 | bytes 5243909 | tf_op jit(solution)/shard_map/while/body/eval_jaxpr/ps,pac->sac/dot_general | solution.py:34
  132.9 2.9 %gather_fusion = bf16[16,256,256]{2,1,0:T(8,128)(2,1)S(1)} fusion(bf16[32,256,256]{2,1,0:T(8,128)(2,1)} %get-tuple-element.180, s32[1024]{0:T(1024)S(1)} %pad_clamp_fusion.3), kind=kCustom, calls=%fused_computation.clone.clone.1 | custom fusion | bytes 4194368 | tf_op jit(solution)/shard_map/while/body/eval_jaxpr/gather | solution.py:29
  135.7 5.4 %gather_fusion.1 = bf16[16,256,256]{2,1,0:T(8,128)(2,1)} fusion(bf16[32,2,256,256]{3,2,1,0:T(8,128)(2,1)} %get-tuple-element.183, s32[16]{0:T(128)S(1)} %get-tuple-element.155), kind=kCustom, calls=%fused_computation.1.clone.clone.1 | custom fusion | bytes 4194432 | tf_op jit(solution)/shard_map/while/body/eval_jaxpr/gather | solution.py:30
  141.2 4.3 %fusion.28 = f32[16,256,256]{2,1,0:T(8,128)} fusion(bf16[16,256,256]{2,1,0:T(8,128)(2,1)S(1)} %gather_fusion, bf16[16,256,256]{2,1,0:T(8,128)(2,1)} %gather_fusion.1), kind=kOutput, calls=%fused_computation.42.clone.1 | convolution fusion | flops 536870912 | bytes 8388608 | tf_op jit(solution)/shard_map/while/body/eval_jaxpr/pab,pbc->pac/dot_general | solution.py:31
  145.4 7.2 %fusion.29 = f32[2,256,256]{2,0,1:T(2,128)S(1)} fusion(f32[16,256,256]{2,1,0:T(8,128)} %fusion.28, f32[2,256,256]{2,0,1:T(2,128)S(1)} %get-tuple-element.167, pred[]{:T(512)S(6)} %compare.10, f32[4,16,2]{1,2,0:T(2,128)S(1)} %get-tuple-element.178, s32[]{:T(128)} %get-tuple-element.166), kind=kOutput, calls=%fused_computation.5.clone.1 | convolution fusion | flops 25427968 | bytes 5243909 | tf_op jit(solution)/shard_map/while/body/eval_jaxpr/ps,pac->sac/dot_general | solution.py:34
  152.7 2.9 %gather_fusion = bf16[16,256,256]{2,1,0:T(8,128)(2,1)S(1)} fusion(bf16[32,256,256]{2,1,0:T(8,128)(2,1)} %get-tuple-element.180, s32[1024]{0:T(1024)S(1)} %pad_clamp_fusion.3), kind=kCustom, calls=%fused_computation.clone.clone.1 | custom fusion | bytes 4194368 | tf_op jit(solution)/shard_map/while/body/eval_jaxpr/gather | solution.py:29
  155.5 5.4 %gather_fusion.1 = bf16[16,256,256]{2,1,0:T(8,128)(2,1)} fusion(bf16[32,2,256,256]{3,2,1,0:T(8,128)(2,1)} %get-tuple-element.183, s32[16]{0:T(128)S(1)} %get-tuple-element.155), kind=kCustom, calls=%fused_computation.1.clone.clone.1 | custom fusion | bytes 4194432 | tf_op jit(solution)/shard_map/while/body/eval_jaxpr/gather | solution.py:30
  160.9 4.3 %fusion.28 = f32[16,256,256]{2,1,0:T(8,128)} fusion(bf16[16,256,256]{2,1,0:T(8,128)(2,1)S(1)} %gather_fusion, bf16[16,256,256]{2,1,0:T(8,128)(2,1)} %gather_fusion.1), kind=kOutput, calls=%fused_computation.42.clone.1 | convolution fusion | flops 536870912 | bytes 8388608 | tf_op jit(solution)/shard_map/while/body/eval_jaxpr/pab,pbc->pac/dot_general | solution.py:31
  165.2 7.2 %fusion.29 = f32[2,256,256]{2,0,1:T(2,128)S(1)} fusion(f32[16,256,256]{2,1,0:T(8,128)} %fusion.28, f32[2,256,256]{2,0,1:T(2,128)S(1)} %get-tuple-element.167, pred[]{:T(512)S(6)} %compare.10, f32[4,16,2]{1,2,0:T(2,128)S(1)} %get-tuple-element.178, s32[]{:T(128)} %get-tuple-element.166), kind=kOutput, calls=%fused_computation.5.clone.1 | convolution fusion | flops 25427968 | bytes 5243909 | tf_op jit(solution)/shard_map/while/body/eval_jaxpr/ps,pac->sac/dot_general | solution.py:34
  172.4 0.1 fusion.12
  172.5 0.1 select_reduce_fusion.1
  172.5 0.7 broadcast_in_dim.93
  173.2 11.2 %all-to-all-start.1 = ((f32[32,2,256]{2,1,0:T(2,128)}), f32[32,2,256]{2,1,0:T(2,128)S(1)}, u32[]{:S(2)}, u32[]{:S(2)}) async-start(f32[32,2,256]{2,1,0:T(2,128)} %broadcast_in_dim.93), calls=%async_computation.1 | async-start | bytes 131072 | tf_op jit(solution)/shard_map/all_to_all | solution.py:9
  184.4 14.4 %all-to-all-done.1 = f32[32,2,256]{2,1,0:T(2,128)S(1)} async-done(((f32[32,2,256]{2,1,0:T(2,128)}), f32[32,2,256]{2,1,0:T(2,128)S(1)}, u32[]{:S(2)}, u32[]{:S(2)}) %all-to-all-start.1) | async-done | bytes 65568 | tf_op jit(solution)/shard_map/all_to_all | solution.py:9
  198.9 0.1 select_reduce_fusion
  199.0 0.1 broadcast_select_fusion
  199.0 0.0 copy-done
  199.0 0.9 select_bitcast_fusion
  (20 shorter events, 0.2 us)
Async XLA Ops:
  6.5 86.7 %all-gather.3.cloned.1.call-start = ((), (), s32[]{:S(2)}) async-start(), calls=%async_computation.2 | async-start | bytes 8650752 | tf_op jit(solution)/shard_map/all_gather | solution.py:65
  10.6 10.3 %copy-start.1 = (s32[1,2]{1,0:T(1,128)S(1)}, s32[1,2]{1,0:T(1,128)}, u32[]{:S(2)}) copy-start(s32[1,2]{1,0:T(1,128)} %param.6) | copy-start | bytes 28
  10.6 44.3 %copy-start.2 = (s32[64,2]{0,1:T(2,128)S(1)}, s32[64,2]{0,1:T(2,128)}, u32[]{:S(2)}) copy-start(s32[64,2]{0,1:T(2,128)} %param.7) | copy-start | bytes 1540
  10.6 72.5 %all-to-all-start = ((bf16[16,1,2,256,256]{4,3,2,1,0:T(8,128)(2,1)}), bf16[16,1,2,256,256]{4,3,2,1,0:T(8,128)(2,1)}, u32[]{:S(2)}, u32[]{:S(2)}) async-start(bf16[16,1,2,256,256]{4,3,2,1,0:T(8,128)(2,1)} %stack.2), calls=%async_computation | async-start | bytes 8388608 | tf_op jit(solution)/shard_map/all_to_all | solution.py:49
  93.2 105.8 %copy-start = (bf16[1,2,256,256]{3,2,1,0:T(8,128)(2,1)S(1)}, bf16[1,2,256,256]{3,2,1,0:T(8,128)(2,1)}, u32[]{:S(2)}) copy-start(bf16[1,2,256,256]{3,2,1,0:T(8,128)(2,1)} %param.5) | copy-start | bytes 786436
  173.2 25.6 %all-to-all-start.1 = ((f32[32,2,256]{2,1,0:T(2,128)}), f32[32,2,256]{2,1,0:T(2,128)S(1)}, u32[]{:S(2)}, u32[]{:S(2)}) async-start(f32[32,2,256]{2,1,0:T(2,128)} %broadcast_in_dim.93), calls=%async_computation.1 | async-start | bytes 131072 | tf_op jit(solution)/shard_map/all_to_all | solution.py:9
Sparse Core Ops, SparseCore 0:
  9.5 83.7 all-gather.2
